TPU v7x, 32 devices: a whole 2x2x4 slice. The times are simulated.
32 devices in a mesh: segment: 2 (over core), expert: 16 (over z, y, x).
Axes of the slice: x: 2, y: 2, z: 4, core: 2. Of those that a mesh axis runs over, the one named last changes fastest.
Arguments:
- tokens: bfloat16 [2, 1024, 2048], P(None, 'expert'), may hold values from -6 to 6
- routing: int32 [2, 2, 1024, 8], P(None, None, 'expert'), may hold values from 0 to 15, all different within a row; in each aligned block of 64 rows (0 to 63, 64 to 127, ..., all dimensions but the last counted through in order) at most 64 rows name the same one
- norm_gain: bfloat16 [2, 2048], P('segment'), may hold values from 0.5 to 1.5
- router_weight: bfloat16 [2, 2048, 16], P('segment'), may hold values from -0.125 to 0.125
- expert_gate_up: bfloat16 [2, 16, 2048, 768], P('segment', 'expert'), may hold values from -0.125 to 0.125
- expert_down: bfloat16 [2, 16, 384, 2048], P('segment', 'expert'), may hold values from -0.3125 to 0.3125
- pair_index: int32 [64], replicated, may hold values from 0 to 63, each once
- topic_ids: int32 [64], replicated, may hold values from 0 to 7
Outputs:
- final_hidden: bfloat16 [2, 1024, 2048], P('segment', 'expert')
- query_loss: float32 [64], P(('segment', 'expert'))
Inputs may be any that keep to these rules, and one draw needn't show every extreme that they name: `routing`: each row names 8 different experts. In the rows of one device (each aligned block of 64 token rows of one layer and micro-batch) no expert is named by more than 64 rows, a bound that some block reaches. `pair_index`: every passage is the positive of exactly one query.
All inputs are finite; a program needn't handle non-finite values.
Results may differ from a plain program's by a relative error of at most 0.0059.
Values may be sent and summed in bfloat16 or wider, within the bound.
A program may use at most 128 MiB of HBM per device.

v0:
```python
import jax
import jax.numpy as jnp
from jax import lax
from jax.sharding import PartitionSpec as P

SEQ = 16
EPSILON = 1e-06
SOFTMAX_WARMTH = 0.05


def passed_along(block, axis, distance):
    devices = range(lax.axis_size(axis))
    route = [(i - distance, i) for i in devices if i - distance in devices]
    return lax.ppermute(block, axis, route)


def expert_block(received, gate_up, down_proj):
    source_count, slot_count, model_width = received.shape
    flat_rows = received.reshape(source_count * slot_count, model_width)
    projected = jnp.dot(flat_rows, gate_up, preferred_element_type=jnp.float32)
    half_width = gate_up.shape[1] // 2
    hidden = (jax.nn.silu(projected[:, :half_width]) * projected[:, half_width:]).astype(
        jnp.bfloat16
    )
    result = jnp.dot(hidden, down_proj, preferred_element_type=jnp.float32).astype(jnp.bfloat16)
    return result.reshape(source_count, slot_count, model_width)


def moe_layer(inputs, routes, norm_gain, router_weight, gate_up, down_proj):
    row_count, model_width = inputs.shape
    top_count = routes.shape[1]
    expert_count = router_weight.shape[1]
    capacity = 2 * row_count * top_count // expert_count
    widened = inputs.astype(jnp.float32)
    normed = (
        widened
        * lax.rsqrt(jnp.mean(widened * widened, axis=1, keepdims=True) + EPSILON)
        * norm_gain.astype(jnp.float32)
    ).astype(jnp.bfloat16)
    similarity_logits = jnp.dot(normed, router_weight, preferred_element_type=jnp.float32)
    chosen = jnp.take_along_axis(similarity_logits, routes, axis=1)
    raised = jnp.exp(chosen)
    gate_weights = raised / jnp.sum(raised, axis=1, keepdims=True)
    flat_ids = routes.reshape(-1)
    one_hot = (flat_ids[:, None] == jnp.arange(expert_count, dtype=jnp.int32)[None, :]).astype(
        jnp.int32
    )
    earlier = jnp.cumsum(one_hot, axis=0) - one_hot
    slot_index = jnp.sum(earlier * one_hot, axis=1)
    target = flat_ids * capacity + slot_index
    repeated = jnp.repeat(normed, top_count, axis=0)
    outgoing = (
        jnp.zeros((expert_count * capacity, model_width), jnp.bfloat16).at[target].set(repeated)
    )
    outgoing = outgoing.reshape(expert_count, capacity, model_width)
    answered = expert_block(
        lax.all_to_all(outgoing, "expert", split_axis=0, concat_axis=0, tiled=True),
        gate_up,
        down_proj,
    )
    returned = lax.all_to_all(answered, "expert", split_axis=0, concat_axis=0, tiled=True)
    picked = returned.reshape(expert_count * capacity, model_width)[target].astype(jnp.float32)
    picked = picked.reshape(row_count, top_count, model_width)
    mixture = jnp.sum(picked * gate_weights[:, :, None], axis=1)
    return (widened + mixture).astype(jnp.bfloat16)


def pooled_embeddings(final_rows):
    widened = final_rows.astype(jnp.float32)
    pooled = jnp.mean(widened.reshape(-1, SEQ, widened.shape[1]), axis=1)
    return (pooled * lax.rsqrt(jnp.sum(pooled * pooled, axis=1, keepdims=True) + EPSILON)).astype(
        jnp.bfloat16
    )


def local(
    tokens, routing, norm_gain, router_weight, expert_gate_up, expert_down, pair_index, topic_ids
):
    segment_index = lax.axis_index("segment")
    micro_count = tokens.shape[0]
    segment_routes = lax.dynamic_index_in_dim(routing, segment_index, 0, keepdims=False)
    carried = jnp.zeros_like(tokens[0])
    finished = []
    for time_step in range(micro_count + 1):
        fresh_rows = tokens[min(time_step, micro_count - 1)]
        segment_input = jnp.where(segment_index == 0, fresh_rows, carried)
        micro_pick = jnp.clip(time_step - segment_index, 0, micro_count - 1)
        layer_routes = lax.dynamic_index_in_dim(segment_routes, micro_pick, 0, keepdims=False)
        produced = moe_layer(
            segment_input,
            layer_routes,
            norm_gain[0],
            router_weight[0],
            expert_gate_up[0, 0],
            expert_down[0, 0],
        )
        finished.append(produced)
        if time_step < micro_count:
            carried = passed_along(produced, "segment", 1)
    sent_back = passed_along(finished[1], "segment", -1)
    final_rows = jnp.where(segment_index == 0, sent_back, finished[micro_count])
    embedded = pooled_embeddings(final_rows)
    half_count = embedded.shape[0] // 2
    query_vectors = embedded[:half_count]
    passage_vectors = embedded[half_count:]
    device_flat = lax.axis_index(("segment", "expert"))
    columns = jnp.arange(topic_ids.shape[0], dtype=jnp.int32)
    matched = pair_index[:, None] == columns[None, :]
    positive_topic = jnp.sum(
        jnp.where(matched, topic_ids[None, :], jnp.zeros_like(topic_ids)[None, :]), axis=1
    )
    every_query_row = lax.all_gather(query_vectors, ("segment", "expert"), axis=0, tiled=True)
    local_ids = device_flat * half_count + jnp.arange(half_count, dtype=jnp.int32)
    local_topics = lax.dynamic_slice_in_dim(topic_ids, device_flat * half_count, half_count)
    pair_scores = (
        jnp.dot(every_query_row, passage_vectors.T, preferred_element_type=jnp.float32)
        / SOFTMAX_WARMTH
    )
    is_positive = pair_index[:, None] == local_ids[None, :]
    kept_pairs = is_positive | (local_topics[None, :] != positive_topic[:, None])
    partition_part = jnp.sum(
        jnp.where(kept_pairs, jnp.exp(pair_scores), jnp.zeros_like(pair_scores)), axis=1
    )
    positive_part = jnp.sum(
        jnp.where(is_positive, pair_scores, jnp.zeros_like(pair_scores)), axis=1
    )
    partition, positive = (
        lax.psum_scatter(partition_part, ("segment", "expert"), scatter_dimension=0, tiled=True),
        lax.psum_scatter(positive_part, ("segment", "expert"), scatter_dimension=0, tiled=True),
    )
    query_loss = jnp.log(partition) - positive
    return (final_rows[None], query_loss)


def solution(mesh):
    in_specs = (
        P(None, "expert", None),
        P(None, None, "expert", None),
        P("segment", None),
        P("segment", None, None),
        P("segment", "expert", None, None),
        P("segment", "expert", None, None),
        P(),
        P(),
    )
    out_specs = (P("segment", "expert", None), P(("segment", "expert")))
    return jax.shard_map(local, mesh=mesh, in_specs=in_specs, out_specs=out_specs, check_vma=False)
```

profile of v0, /device:TPU:14, one launch (start us, length us, event | category | flops | bytes accessed | tf_op | source)
XLA Modules:
  0.0 794.9 jit_solution(5908741902070264360)
XLA Ops:
  0.7 0.9 bitcast_or_fusion
  1.8 1.2 reduce-window.20
  3.4 1.1 fusion.36
  5.4 1.1 fusion.38
  6.5 6.2 scatter_custom_fusion
  12.6 98.8 %all_to_all.30 = bf16[16,64,2048]{2,1,0:T(8,128)(2,1)S(1)} all-to-all(bf16[16,64,2048]{2,1,0:T(8,128)(2,1)} %bitcast.211), channel_id=1, replica_groups=mesh['segment'=2,'expert'=16] {'expert'}, dimensions={0} | all-to-all | bytes 8388608 | tf_op jit(solution)/shard_map/all_to_all | solution.py:57
  111.5 3.4 fusion.7
  114.9 4.3 convolution_convert_fusion.2
  119.2 7.0 all-to-all-start.1
  126.7 1.2 fusion.52
  127.9 3.9 gather_fusion.3
  132.1 1.2 reduce-window.24
  133.5 84.3 %all-to-all-done.1 = bf16[16,64,2048]{2,1,0:T(8,128)(2,1)} async-done(((bf16[16,64,2048]{2,1,0:T(8,128)(2,1)}), bf16[16,64,2048]{2,1,0:T(8,128)(2,1)}, u32[]{:S(2)}, u32[]{:S(2)}) %all-to-all-start.1) | async-done | bytes 4194336 | tf_op jit(solution)/shard_map/all_to_all | solution.py:61
  217.8 8.0 %gather_fusion = bf16[512,2048]{1,0:T(8,128)(2,1)} fusion(bf16[1024,2048]{1,0:T(8,128)(2,1)} %bitcast.12, s32[1024]{0:T(1024)S(1)} %pad_clamp_fusion.2), kind=kCustom, calls=%fused_computation.3 | custom fusion | bytes 4196352 | tf_op jit(solution)/shard_map/gather | solution.py:62
  225.8 3.4 fusion.2
  229.2 1.7 fusion.39
  230.9 1.3 collective-permute-start
  232.5 1.1 collective-permute-done
  233.6 1.1 fusion.42
  235.6 6.2 scatter_custom_fusion.1
  241.7 97.5 %all_to_all.31 = bf16[16,64,2048]{2,1,0:T(8,128)(2,1)S(1)} all-to-all(bf16[16,64,2048]{2,1,0:T(8,128)(2,1)} %bitcast.213), channel_id=1, replica_groups=mesh['segment'=2,'expert'=16] {'expert'}, dimensions={0} | all-to-all | bytes 8388608 | tf_op jit(solution)/shard_map/all_to_all | solution.py:57
  339.3 3.4 fusion.5
  342.7 4.3 convolution_convert_fusion.1
  347.1 6.3 all-to-all-start.3
  354.4 2.2 reduce-window.26
  357.1 3.9 gather_fusion.4
  361.9 83.8 %all-to-all-done.3 = bf16[16,64,2048]{2,1,0:T(8,128)(2,1)} async-done(((bf16[16,64,2048]{2,1,0:T(8,128)(2,1)}), bf16[16,64,2048]{2,1,0:T(8,128)(2,1)}, u32[]{:S(2)}, u32[]{:S(2)}) %all-to-all-start.3) | async-done | bytes 4194336 | tf_op jit(solution)/shard_map/all_to_all | solution.py:61
  445.7 8.0 %gather_fusion.1 = bf16[512,2048]{1,0:T(8,128)(2,1)} fusion(bf16[1024,2048]{1,0:T(8,128)(2,1)} %bitcast.25, s32[1024]{0:T(1024)S(1)} %pad_clamp_fusion.1), kind=kCustom, calls=%fused_computation.4 | custom fusion | bytes 4196352 | tf_op jit(solution)/shard_map/gather | solution.py:62
  453.7 3.4 fusion.1
  457.9 2.4 collective-permute-start.2
  460.7 1.1 fusion.46
  461.9 0.8 fusion.48
  462.7 6.6 scatter_custom_fusion.2
  469.3 97.4 %all_to_all.32 = bf16[16,64,2048]{2,1,0:T(8,128)(2,1)S(1)} all-to-all(bf16[16,64,2048]{2,1,0:T(8,128)(2,1)} %bitcast.212), channel_id=1, replica_groups=mesh['segment'=2,'expert'=16] {'expert'}, dimensions={0} | all-to-all | bytes 8388608 | tf_op jit(solution)/shard_map/all_to_all | solution.py:57
  566.7 3.4 fusion.3
  570.1 4.3 convolution_convert_fusion
  574.5 6.3 all-to-all-start.5
  581.3 1.5 collective-permute-start.1
  582.7 1.1 fusion.56
  583.9 3.9 gather_fusion.5
  588.1 85.2 %all-to-all-done.5 = bf16[16,64,2048]{2,1,0:T(8,128)(2,1)} async-done(((bf16[16,64,2048]{2,1,0:T(8,128)(2,1)}), bf16[16,64,2048]{2,1,0:T(8,128)(2,1)}, u32[]{:S(2)}, u32[]{:S(2)}) %all-to-all-start.5) | async-done | bytes 4194336 | tf_op jit(solution)/shard_map/all_to_all | solution.py:61
  673.3 8.0 %gather_fusion.2 = bf16[512,2048]{1,0:T(8,128)(2,1)} fusion(bf16[1024,2048]{1,0:T(8,128)(2,1)} %bitcast.36, s32[1024]{0:T(1024)S(1)} %pad_clamp_fusion), kind=kCustom, calls=%fused_computation.5 | custom fusion | bytes 4196352 | tf_op jit(solution)/shard_map/gather | solution.py:62
  681.3 3.4 fusion
  684.8 1.8 convert_reduce_fusion
  686.8 57.1 %all-gather = bf16[32,2,2048]{2,1,0:T(2,128)(2,1)S(1)} all-gather(bf16[1,2,2048]{2,1,0:T(2,128)(2,1)S(1)} %slice_bitcast_fusion), channel_id=1, replica_groups=mesh['segment'=2,'expert'=16] {'segment','expert'}, dimensions={0}, use_global_device_ids=true | all-gather | bytes 270336 | tf_op jit(solution)/shard_map/all_gather | solution.py:112
  743.9 0.8 reshape.399
  744.7 1.1 fusion.76
  745.8 48.3 %all-reduce.2 = (f32[64]{0:T(128)S(1)}, f32[64]{0:T(128)S(1)}) all-reduce(f32[64]{0:T(128)S(1)} %get-tuple-element.4, f32[64]{0:T(128)S(1)} %get-tuple-element.3), channel_id=3, replica_groups=mesh['segment'=2,'expert'=16] {'segment','expert'}, use_global_device_ids=true, to_apply=%region_27.29.clone | all-reduce | flops 128 | bytes 1024
  (97 shorter events, 8.7 us)
Async XLA Ops:
  0.6 110.8 %copy-start = (bf16[1,1,2048,768]{3,2,1,0:T(8,128)(2,1)S(1)}, bf16[1,1,2048,768]{3,2,1,0:T(8,128)(2,1)}, u32[]{:S(2)}) copy-start(bf16[1,1,2048,768]{3,2,1,0:T(8,128)(2,1)} %param.14) | copy-start | bytes 9437188
  111.5 3.4 copy-start.5
  119.2 7.4 copy-start.3
  119.2 98.5 %all-to-all-start.1 = ((bf16[16,64,2048]{2,1,0:T(8,128)(2,1)}), bf16[16,64,2048]{2,1,0:T(8,128)(2,1)}, u32[]{:S(2)}, u32[]{:S(2)}) async-start(bf16[16,64,2048]{2,1,0:T(8,128)(2,1)} %bitcast.215), calls=%async_computation.1 | async-start | bytes 8388608 | tf_op jit(solution)/shard_map/all_to_all | solution.py:61
  230.9 2.6 collective-permute-start
  234.7 0.7 copy-start.1
  339.3 3.4 copy-start.6
  347.1 98.6 %all-to-all-start.3 = ((bf16[16,64,2048]{2,1,0:T(8,128)(2,1)}), bf16[16,64,2048]{2,1,0:T(8,128)(2,1)}, u32[]{:S(2)}, u32[]{:S(2)}) async-start(bf16[16,64,2048]{2,1,0:T(8,128)(2,1)} %bitcast.216), calls=%async_computation.3 | async-start | bytes 8388608 | tf_op jit(solution)/shard_map/all_to_all | solution.py:61
  356.9 4.1 copy-start.4
  445.7 11.5 %copy-start.2 = (bf16[64,2048]{1,0:T(8,128)(2,1)S(1)}, bf16[64,2048]{1,0:T(8,128)(2,1)}, u32[]{:S(2)}) copy-start(bf16[64,2048]{1,0:T(8,128)(2,1)} %copy-done.1) | copy-start | bytes 786436
  453.7 6.6 slice-start
  457.9 2.8 collective-permute-start.2
  566.7 3.4 copy-start.7
  574.5 6.5 copy-start.8
  574.5 6.6 copy-start.9
  574.5 98.8 %all-to-all-start.5 = ((bf16[16,64,2048]{2,1,0:T(8,128)(2,1)}), bf16[16,64,2048]{2,1,0:T(8,128)(2,1)}, u32[]{:S(2)}, u32[]{:S(2)}) async-start(bf16[16,64,2048]{2,1,0:T(8,128)(2,1)} %bitcast.214), calls=%async_computation.5 | async-start | bytes 8388608 | tf_op jit(solution)/shard_map/all_to_all | solution.py:61
  581.3 103.5 %collective-permute-start.1 = (bf16[64,2048]{1,0:T(8,128)(2,1)}, bf16[64,2048]{1,0:T(8,128)(2,1)}, u32[]{:S(2)}, u32[]{:S(2)}) collective-permute-start(bf16[64,2048]{1,0:T(8,128)(2,1)} %fusion.45), channel_id=1, source_target_pairs={{16,0},{17,1},{18,2},{19,3},{20,4},{21,5},{22,6},{23,7},{24,8},{25... | collective-permute-start | bytes 786440 | tf_op jit(solution)/shard_map/ppermute | solution.py:14
where the time goes:
time: 804 us; the launch traced here: 795 us
  blocking collectives  399 us (50%)
  waiting for transfers between devices  254 us (32%)
  local copies, waits for them, and re-layouts  60.1 us (7%)
  other arithmetic  28.4 us (4%)
  matrix products  26.9 us (3%)
  starting transfers between devices  24.7 us (3%)
    all_to_all x3, blocking collectives, moe_layer(): lax.all_to_all(outgoing, 'expert', split_axis=0, concat_axis=0, tiled=True)  294 us
    all_to_all x3, waiting for transfers between devices, moe_layer(): lax.all_to_all(answered, 'expert', split_axis=0, concat_axis=0, tiled=True)  253 us
    all_gather x1, blocking collectives, local(): lax.all_gather(query_vectors, ('segment', 'expert'), axis=0, tiled=True)  57.1 us
    unnamed x1, blocking collectives  48.3 us
    gather x3, local copies, waits for them, and re-layouts, moe_layer(): returned.reshape(expert_count * capacity, model_width)[target]  24 us
    all_to_all x3, starting transfers between devices, moe_layer(): lax.all_to_all(answered, 'expert', split_axis=0, concat_axis=0, tiled=True)  19.6 us
    scatter x3, local copies, waits for them, and re-layouts, moe_layer(): jnp.zeros((expert_count * capacity, model_width), jnp.bfloat16).at[target]  18.9 us
  transfers between devices with their start and end apart: 6, of which 5 were waited for; matrix products, arithmetic and copies ran while one was open for 4% of the time, Pallas kernels for 0%

commit v1 on v0

--- a/solution.py
+++ b/solution.py
@@ -58,7 +58,24 @@
         gate_up,
         down_proj,
     )
-    returned = lax.all_to_all(answered, "expert", split_axis=0, concat_axis=0, tiled=True)
+
+    def register_the_squares(original, chip_axis):
+        taken_in, placed = (lax.axis_size(chip_axis), lax.axis_index(chip_axis))
+        item_now = original.shape[0] // taken_in
+        ready = jnp.roll(original, -placed * item_now, 0)
+        heap = [lax.slice_in_dim(ready, 0, item_now, axis=0)]
+        for dd in range(1, taken_in):
+            raw_out = lax.slice_in_dim(ready, dd * item_now, (dd + 1) * item_now, axis=0)
+            heap.append(
+                lax.ppermute(
+                    raw_out, chip_axis, [(it, (it + dd) % taken_in) for it in range(taken_in)]
+                )
+            )
+        w2 = jnp.concatenate(heap[::-1], 0)
+        piece_next = jnp.roll(w2, (placed + 1) * heap[0].shape[0], 0)
+        return piece_next
+
+    returned = register_the_squares(answered, "expert")
     picked = returned.reshape(expert_count * capacity, model_width)[target].astype(jnp.float32)
     picked = picked.reshape(row_count, top_count, model_width)
     mixture = jnp.sum(picked * gate_weights[:, :, None], axis=1)

time: 804 us -> 892 us (1.11)
  blocking collectives: 399 us -> 116 us
  starting transfers between devices: 24.7 us -> 282 us
  waiting for transfers between devices: 254 us -> 325 us
  local copies, waits for them, and re-layouts: 60.1 us -> 83.3 us
  other arithmetic: 28.4 us -> 47 us
    all_to_all x3 -> x0, blocking collectives: 294 us -> none  [moe_layer(): lax.all_to_all(outgoing, 'expert', split_axis=0, concat_axis=0, tiled=True)]
    ppermute x0 -> x45, starting transfers between devices: none -> 251 us  [register_the_squares(): lax.ppermute(raw_out, chip_axis, [(it, (it + dd) % taken_in) for it in ra...]
    ppermute x0 -> x45, waiting for transfers between devices: none -> 59.1 us  [register_the_squares(): lax.ppermute(raw_out, chip_axis, [(it, (it + dd) % taken_in) for it in ra...]
    concatenate x0 -> x6, other arithmetic: none -> 13.3 us  [the longest x3 8.6 us: register_the_squares(): piece_next = jnp.roll(w2, (placed + 1) * heap[0].shape[0], 0)]
    unnamed x22 -> x103, local copies, waits for them, and re-layouts: 1.53 us -> 14 us
    all_gather x1, blocking collectives: 57.1 us -> 69.3 us  [local(): lax.all_gather(query_vectors, ('segment', 'expert'), axis=0, tiled=True)]
    all_to_all x3, waiting for transfers between devices: 253 us -> 265 us  [moe_layer(): lax.all_to_all(outgoing, 'expert', split_axis=0, concat_axis=0, tiled=True)]
  transfers between devices with their start and end apart: 6 -> 51, of which waited for: 5 -> 21; matrix products, arithmetic and copies ran while one was open for 4% -> 7% of each run, Pallas kernels for 0% -> 0%
where the time goes in v1:
time: 892 us; the launch traced here: 882 us
  waiting for transfers between devices  325 us (36%)
  starting transfers between devices  282 us (32%)
  blocking collectives  116 us (13%)
  local copies, waits for them, and re-layouts  83.3 us (9%)
  other arithmetic  47 us (5%)
  matrix products  26.7 us (3%)
    all_to_all x3, waiting for transfers between devices, moe_layer(): lax.all_to_all(outgoing, 'expert', split_axis=0, concat_axis=0, tiled=True)  265 us
    ppermute x45, starting transfers between devices, register_the_squares(): lax.ppermute(raw_out, chip_axis, [(it, (it + dd) % taken_in) for it in ra...  251 us
    all_gather x1, blocking collectives, local(): lax.all_gather(query_vectors, ('segment', 'expert'), axis=0, tiled=True)  69.3 us
    ppermute x45, waiting for transfers between devices, register_the_squares(): lax.ppermute(raw_out, chip_axis, [(it, (it + dd) % taken_in) for it in ra...  59.1 us
    unnamed x1, blocking collectives  46.5 us
    all_to_all x3, starting transfers between devices, moe_layer(): lax.all_to_all(outgoing, 'expert', split_axis=0, concat_axis=0, tiled=True)  26.4 us
    gather x3, local copies, waits for them, and re-layouts, moe_layer(): returned.reshape(expert_count * capacity, model_width)[target]  24 us
    scatter x3, local copies, waits for them, and re-layouts, moe_layer(): jnp.zeros((expert_count * capacity, model_width), jnp.bfloat16).at[target]  19.4 us
  transfers between devices with their start and end apart: 51, of which 21 were waited for; matrix products, arithmetic and copies ran while one was open for 7% of the time, Pallas kernels for 0%

profile of v1, /device:TPU:14, one launch (start us, length us, event | category | flops | bytes accessed | tf_op | source)
XLA Modules:
  0.0 882.3 jit_solution(17860870679141251009)
XLA Ops:
  7.1 6.2 scatter_custom_fusion
  13.3 7.3 all-to-all-start
  22.0 3.9 gather_fusion.3
  27.5 87.8 %all-to-all-done = bf16[16,64,2048]{2,1,0:T(8,128)(2,1)} async-done(((bf16[16,64,2048]{2,1,0:T(8,128)(2,1)}), bf16[16,64,2048]{2,1,0:T(8,128)(2,1)}, u32[]{:S(2)}, u32[]{:S(2)}) %all-to-all-start) | async-done | bytes 4194336 | tf_op jit(solution)/shard_map/all_to_all | solution.py:57
  115.3 5.3 fusion.13
  135.5 4.1 collective-permute-start.3
  147.2 3.8 collective-permute-start.7
  151.0 4.0 collective-permute-start.8
  155.1 5.0 collective-permute-done.4
  160.1 38.7 %collective-permute-start.9 = (bf16[1,64,2048]{2,1,0:T(8,128)(2,1)}, bf16[1,64,2048]{2,1,0:T(8,128)(2,1)S(1)}, u32[]{:S(2)}, u32[]{:S(2)}) collective-permute-start(bf16[1,64,2048]{2,1,0:T(8,128)(2,1)} %get-tuple-element.55), channel_id=1, source_target_pairs={{0,6},{1,7},{2,8},{3,9},{4,10},{5,11},{6,12},{7,13},{8,14},{9,15},... | collective-permute-start | bytes 786440 | tf_op jit(solution)/shard_map/ppermute | solution.py:70
  199.0 7.9 collective-permute-start.12
  207.0 11.2 %collective-permute-start.13 = (bf16[1,64,2048]{2,1,0:T(8,128)(2,1)S(1)}, bf16[1,64,2048]{2,1,0:T(8,128)(2,1)S(1)}, u32[]{:S(2)}, u32[]{:S(2)}) collective-permute-start(bf16[1,64,2048]{2,1,0:T(8,128)(2,1)S(1)} %copy-done.6), channel_id=1, source_target_pairs={{0,2},{1,3},{2,4},{3,5},{4,6},{5,7},{6,8},{7,9},{8,10},{9,11},{10,... | collective-permute-start | bytes 786440 | tf_op jit(solution)/shard_map/ppermute | solution.py:70
  218.2 7.0 collective-permute-start.14
  239.5 8.0 gather_fusion
  247.4 3.4 fusion.8
  257.3 6.6 scatter_custom_fusion.1
  263.9 8.3 all-to-all-start.1
  276.0 3.9 gather_fusion.4
  280.1 88.1 %all-to-all-done.1 = bf16[16,64,2048]{2,1,0:T(8,128)(2,1)} async-done(((bf16[16,64,2048]{2,1,0:T(8,128)(2,1)}), bf16[16,64,2048]{2,1,0:T(8,128)(2,1)}, u32[]{:S(2)}, u32[]{:S(2)}) %all-to-all-start.1) | async-done | bytes 4194336 | tf_op jit(solution)/shard_map/all_to_all | solution.py:57
  368.2 5.3 fusion.11
  382.0 4.2 collective-permute-start.19
  387.2 8.4 collective-permute-done.16
  405.8 6.0 collective-permute-done.20
  411.8 36.6 %collective-permute-start.25 = (bf16[1,64,2048]{2,1,0:T(8,128)(2,1)}, bf16[1,64,2048]{2,1,0:T(8,128)(2,1)S(1)}, u32[]{:S(2)}, u32[]{:S(2)}) collective-permute-start(bf16[1,64,2048]{2,1,0:T(8,128)(2,1)} %get-tuple-element.40), channel_id=1, source_target_pairs={{0,6},{1,7},{2,8},{3,9},{4,10},{5,11},{6,12},{7,13},{8,14},{9,15},... | collective-permute-start | bytes 786440 | tf_op jit(solution)/shard_map/ppermute | solution.py:70
  448.7 19.1 %collective-permute-start.28 = (bf16[1,64,2048]{2,1,0:T(8,128)(2,1)}, bf16[1,64,2048]{2,1,0:T(8,128)(2,1)S(1)}, u32[]{:S(2)}, u32[]{:S(2)}) collective-permute-start(bf16[1,64,2048]{2,1,0:T(8,128)(2,1)} %get-tuple-element.37), channel_id=1, source_target_pairs={{0,3},{1,4},{2,5},{3,6},{4,7},{5,8},{6,9},{7,10},{8,11},{9,12},{10... | collective-permute-start | bytes 786440 | tf_op jit(solution)/shard_map/ppermute | solution.py:70
  467.9 5.6 collective-permute-start.29
  473.5 7.2 collective-permute-start.30
  482.1 4.5 collective-permute-done.29
  486.6 4.2 collective-permute-done.30
  494.7 8.0 gather_fusion.1
  502.8 3.4 fusion.7
  511.8 6.6 scatter_custom_fusion.2
  518.4 10.8 %all-to-all-start.2 = ((bf16[16,64,2048]{2,1,0:T(8,128)(2,1)}), bf16[16,64,2048]{2,1,0:T(8,128)(2,1)}, u32[]{:S(2)}, u32[]{:S(2)}) async-start(bf16[16,64,2048]{2,1,0:T(8,128)(2,1)} %bitcast.215), calls=%async_computation.2 | async-start | bytes 8388608 | tf_op jit(solution)/shard_map/all_to_all | solution.py:57
  532.3 3.9 gather_fusion.5
  536.4 89.0 %all-to-all-done.2 = bf16[16,64,2048]{2,1,0:T(8,128)(2,1)} async-done(((bf16[16,64,2048]{2,1,0:T(8,128)(2,1)}), bf16[16,64,2048]{2,1,0:T(8,128)(2,1)}, u32[]{:S(2)}, u32[]{:S(2)}) %all-to-all-start.2) | async-done | bytes 4194336 | tf_op jit(solution)/shard_map/all_to_all | solution.py:57
  625.3 5.3 fusion.9
  638.7 4.3 collective-permute-start.36
  643.1 9.8 %collective-permute-done.33 = bf16[1,64,2048]{2,1,0:T(8,128)(2,1)} collective-permute-done((bf16[1,64,2048]{2,1,0:T(8,128)(2,1)}, bf16[1,64,2048]{2,1,0:T(8,128)(2,1)}, u32[]{:S(2)}, u32[]{:S(2)}) %collective-permute-start.33) | collective-permute-done | bytes 262176 | tf_op jit(solution)/shard_map/ppermute | solution.py:70
  655.1 6.8 collective-permute-start.39
  661.9 17.0 %collective-permute-start.40 = (bf16[1,64,2048]{2,1,0:T(8,128)(2,1)}, bf16[1,64,2048]{2,1,0:T(8,128)(2,1)S(1)}, u32[]{:S(2)}, u32[]{:S(2)}) collective-permute-start(bf16[1,64,2048]{2,1,0:T(8,128)(2,1)} %get-tuple-element.27), channel_id=1, source_target_pairs={{0,8},{1,9},{2,10},{3,11},{4,12},{5,13},{6,14},{7,15},{8,0},{9,1},... | collective-permute-start | bytes 786440 | tf_op jit(solution)/shard_map/ppermute | solution.py:70
  679.1 18.2 %collective-permute-start.42 = (bf16[1,64,2048]{2,1,0:T(8,128)(2,1)}, bf16[1,64,2048]{2,1,0:T(8,128)(2,1)S(1)}, u32[]{:S(2)}, u32[]{:S(2)}) collective-permute-start(bf16[1,64,2048]{2,1,0:T(8,128)(2,1)} %get-tuple-element.25), channel_id=1, source_target_pairs={{0,6},{1,7},{2,8},{3,9},{4,10},{5,11},{6,12},{7,13},{8,14},{9,15},... | collective-permute-start | bytes 786440 | tf_op jit(solution)/shard_map/ppermute | solution.py:70
  697.3 19.7 %collective-permute-start.43 = (bf16[1,64,2048]{2,1,0:T(8,128)(2,1)}, bf16[1,64,2048]{2,1,0:T(8,128)(2,1)S(1)}, u32[]{:S(2)}, u32[]{:S(2)}) collective-permute-start(bf16[1,64,2048]{2,1,0:T(8,128)(2,1)} %get-tuple-element.24), channel_id=1, source_target_pairs={{0,5},{1,6},{2,7},{3,8},{4,9},{5,10},{6,11},{7,12},{8,13},{9,14},{... | collective-permute-start | bytes 786440 | tf_op jit(solution)/shard_map/ppermute | solution.py:70
  717.2 17.5 %collective-permute-start.46 = (bf16[1,64,2048]{2,1,0:T(8,128)(2,1)S(1)}, bf16[1,64,2048]{2,1,0:T(8,128)(2,1)S(1)}, u32[]{:S(2)}, u32[]{:S(2)}) collective-permute-start(bf16[1,64,2048]{2,1,0:T(8,128)(2,1)S(1)} %copy-done.9), channel_id=1, source_target_pairs={{0,2},{1,3},{2,4},{3,5},{4,6},{5,7},{6,8},{7,9},{8,10},{9,11},{10,... | collective-permute-start | bytes 786440 | tf_op jit(solution)/shard_map/ppermute | solution.py:70
  737.3 5.6 collective-permute-done.46
  750.1 8.0 gather_fusion.2
  758.1 3.4 fusion.6
  763.6 69.3 %all-gather = bf16[32,2,2048]{2,1,0:T(2,128)(2,1)S(1)} all-gather(bf16[1,2,2048]{2,1,0:T(2,128)(2,1)S(1)} %slice_bitcast_fusion), channel_id=1, replica_groups=mesh['segment'=2,'expert'=16] {'segment','expert'}, dimensions={0}, use_global_device_ids=true | all-gather | bytes 270336 | tf_op jit(solution)/shard_map/all_gather | solution.py:129
  834.8 46.5 %all-reduce.2 = (f32[64]{0:T(128)S(1)}, f32[64]{0:T(128)S(1)}) all-reduce(f32[64]{0:T(128)S(1)} %get-tuple-element.5, f32[64]{0:T(128)S(1)} %get-tuple-element.4), channel_id=3, replica_groups=mesh['segment'=2,'expert'=16] {'segment','expert'}, use_global_device_ids=true, to_apply=%region_27.30.clone | all-reduce | flops 128 | bytes 1024
  (278 shorter events, 115.1 us)
Async XLA Ops:
  13.3 101.9 %all-to-all-start = ((bf16[16,64,2048]{2,1,0:T(8,128)(2,1)}), bf16[16,64,2048]{2,1,0:T(8,128)(2,1)}, u32[]{:S(2)}, u32[]{:S(2)}) async-start(bf16[16,64,2048]{2,1,0:T(8,128)(2,1)} %bitcast.214), calls=%async_computation | async-start | bytes 8388608 | tf_op jit(solution)/shard_map/all_to_all | solution.py:57
  128.3 12.4 %collective-permute-start = (bf16[1,64,2048]{2,1,0:T(8,128)(2,1)}, bf16[1,64,2048]{2,1,0:T(8,128)(2,1)}, u32[]{:S(2)}, u32[]{:S(2)}) collective-permute-start(bf16[1,64,2048]{2,1,0:T(8,128)(2,1)} %get-tuple-element.64), channel_id=1, source_target_pairs={{0,15},{1,0},{2,1},{3,2},{4,3},{5,4},{6,5},{7,6},{8,7},{9,8},{10,9... | collective-permute-start | bytes 786440 | tf_op jit(solution)/shard_map/ppermute | solution.py:70
  132.0 12.8 %collective-permute-start.1 = (bf16[1,64,2048]{2,1,0:T(8,128)(2,1)}, bf16[1,64,2048]{2,1,0:T(8,128)(2,1)}, u32[]{:S(2)}, u32[]{:S(2)}) collective-permute-start(bf16[1,64,2048]{2,1,0:T(8,128)(2,1)} %get-tuple-element.63), channel_id=1, source_target_pairs={{0,14},{1,15},{2,0},{3,1},{4,2},{5,3},{6,4},{7,5},{8,6},{9,7},{10,... | collective-permute-start | bytes 786440 | tf_op jit(solution)/shard_map/ppermute | solution.py:70
  135.4 11.8 %collective-permute-start.2 = (bf16[1,64,2048]{2,1,0:T(8,128)(2,1)}, bf16[1,64,2048]{2,1,0:T(8,128)(2,1)S(1)}, u32[]{:S(2)}, u32[]{:S(2)}) collective-permute-start(bf16[1,64,2048]{2,1,0:T(8,128)(2,1)} %get-tuple-element.62), channel_id=1, source_target_pairs={{0,13},{1,14},{2,15},{3,0},{4,1},{5,2},{6,3},{7,4},{8,5},{9,6},{10... | collective-permute-start | bytes 786440 | tf_op jit(solution)/shard_map/ppermute | solution.py:70
  135.5 15.5 %collective-permute-start.3 = (bf16[1,64,2048]{2,1,0:T(8,128)(2,1)}, bf16[1,64,2048]{2,1,0:T(8,128)(2,1)S(1)}, u32[]{:S(2)}, u32[]{:S(2)}) collective-permute-start(bf16[1,64,2048]{2,1,0:T(8,128)(2,1)} %get-tuple-element.61), channel_id=1, source_target_pairs={{0,12},{1,13},{2,14},{3,15},{4,0},{5,1},{6,2},{7,3},{8,4},{9,5},{1... | collective-permute-start | bytes 786440 | tf_op jit(solution)/shard_map/ppermute | solution.py:70
  139.6 20.5 %collective-permute-start.4 = (bf16[1,64,2048]{2,1,0:T(8,128)(2,1)}, bf16[1,64,2048]{2,1,0:T(8,128)(2,1)S(1)}, u32[]{:S(2)}, u32[]{:S(2)}) collective-permute-start(bf16[1,64,2048]{2,1,0:T(8,128)(2,1)} %get-tuple-element.60), channel_id=1, source_target_pairs={{0,11},{1,12},{2,13},{3,14},{4,15},{5,0},{6,1},{7,2},{8,3},{9,4},{... | collective-permute-start | bytes 786440 | tf_op jit(solution)/shard_map/ppermute | solution.py:70
  140.7 58.1 %collective-permute-start.5 = (bf16[1,64,2048]{2,1,0:T(8,128)(2,1)}, bf16[1,64,2048]{2,1,0:T(8,128)(2,1)S(1)}, u32[]{:S(2)}, u32[]{:S(2)}) collective-permute-start(bf16[1,64,2048]{2,1,0:T(8,128)(2,1)} %get-tuple-element.59), channel_id=1, source_target_pairs={{0,10},{1,11},{2,12},{3,13},{4,14},{5,15},{6,0},{7,1},{8,2},{9,3},... | collective-permute-start | bytes 786440 | tf_op jit(solution)/shard_map/ppermute | solution.py:70
  144.8 54.1 %collective-permute-start.6 = (bf16[1,64,2048]{2,1,0:T(8,128)(2,1)}, bf16[1,64,2048]{2,1,0:T(8,128)(2,1)S(1)}, u32[]{:S(2)}, u32[]{:S(2)}) collective-permute-start(bf16[1,64,2048]{2,1,0:T(8,128)(2,1)} %get-tuple-element.58), channel_id=1, source_target_pairs={{0,9},{1,10},{2,11},{3,12},{4,13},{5,14},{6,15},{7,0},{8,1},{9,2},... | collective-permute-start | bytes 786440 | tf_op jit(solution)/shard_map/ppermute | solution.py:70
  147.2 51.8 %collective-permute-start.7 = (bf16[1,64,2048]{2,1,0:T(8,128)(2,1)}, bf16[1,64,2048]{2,1,0:T(8,128)(2,1)S(1)}, u32[]{:S(2)}, u32[]{:S(2)}) collective-permute-start(bf16[1,64,2048]{2,1,0:T(8,128)(2,1)} %get-tuple-element.57), channel_id=1, source_target_pairs={{0,8},{1,9},{2,10},{3,11},{4,12},{5,13},{6,14},{7,15},{8,0},{9,1},... | collective-permute-start | bytes 786440 | tf_op jit(solution)/shard_map/ppermute | solution.py:70
  151.0 55.9 %collective-permute-start.8 = (bf16[1,64,2048]{2,1,0:T(8,128)(2,1)}, bf16[1,64,2048]{2,1,0:T(8,128)(2,1)S(1)}, u32[]{:S(2)}, u32[]{:S(2)}) collective-permute-start(bf16[1,64,2048]{2,1,0:T(8,128)(2,1)} %get-tuple-element.56), channel_id=1, source_target_pairs={{0,7},{1,8},{2,9},{3,10},{4,11},{5,12},{6,13},{7,14},{8,15},{9,0},... | collective-permute-start | bytes 786440 | tf_op jit(solution)/shard_map/ppermute | solution.py:70
  160.1 58.1 %collective-permute-start.9 = (bf16[1,64,2048]{2,1,0:T(8,128)(2,1)}, bf16[1,64,2048]{2,1,0:T(8,128)(2,1)S(1)}, u32[]{:S(2)}, u32[]{:S(2)}) collective-permute-start(bf16[1,64,2048]{2,1,0:T(8,128)(2,1)} %get-tuple-element.55), channel_id=1, source_target_pairs={{0,6},{1,7},{2,8},{3,9},{4,10},{5,11},{6,12},{7,13},{8,14},{9,15},... | collective-permute-start | bytes 786440 | tf_op jit(solution)/shard_map/ppermute | solution.py:70
  198.8 26.5 %collective-permute-start.10 = (bf16[1,64,2048]{2,1,0:T(8,128)(2,1)}, bf16[1,64,2048]{2,1,0:T(8,128)(2,1)S(1)}, u32[]{:S(2)}, u32[]{:S(2)}) collective-permute-start(bf16[1,64,2048]{2,1,0:T(8,128)(2,1)} %get-tuple-element.54), channel_id=1, source_target_pairs={{0,5},{1,6},{2,7},{3,8},{4,9},{5,10},{6,11},{7,12},{8,13},{9,14},{... | collective-permute-start | bytes 786440 | tf_op jit(solution)/shard_map/ppermute | solution.py:70
  198.9 27.9 %collective-permute-start.11 = (bf16[1,64,2048]{2,1,0:T(8,128)(2,1)}, bf16[1,64,2048]{2,1,0:T(8,128)(2,1)S(1)}, u32[]{:S(2)}, u32[]{:S(2)}) collective-permute-start(bf16[1,64,2048]{2,1,0:T(8,128)(2,1)} %get-tuple-element.53), channel_id=1, source_target_pairs={{0,4},{1,5},{2,6},{3,7},{4,8},{5,9},{6,10},{7,11},{8,12},{9,13},{1... | collective-permute-start | bytes 786440 | tf_op jit(solution)/shard_map/ppermute | solution.py:70
  199.0 31.1 %collective-permute-start.12 = (bf16[1,64,2048]{2,1,0:T(8,128)(2,1)}, bf16[1,64,2048]{2,1,0:T(8,128)(2,1)S(1)}, u32[]{:S(2)}, u32[]{:S(2)}) collective-permute-start(bf16[1,64,2048]{2,1,0:T(8,128)(2,1)} %get-tuple-element.52), channel_id=1, source_target_pairs={{0,3},{1,4},{2,5},{3,6},{4,7},{5,8},{6,9},{7,10},{8,11},{9,12},{10... | collective-permute-start | bytes 786440 | tf_op jit(solution)/shard_map/ppermute | solution.py:70
  207.0 25.8 %collective-permute-start.13 = (bf16[1,64,2048]{2,1,0:T(8,128)(2,1)S(1)}, bf16[1,64,2048]{2,1,0:T(8,128)(2,1)S(1)}, u32[]{:S(2)}, u32[]{:S(2)}) collective-permute-start(bf16[1,64,2048]{2,1,0:T(8,128)(2,1)S(1)} %copy-done.6), channel_id=1, source_target_pairs={{0,2},{1,3},{2,4},{3,5},{4,6},{5,7},{6,8},{7,9},{8,10},{9,11},{10,... | collective-permute-start | bytes 786440 | tf_op jit(solution)/shard_map/ppermute | solution.py:70
  218.2 17.4 %collective-permute-start.14 = (bf16[1,64,2048]{2,1,0:T(8,128)(2,1)S(1)}, bf16[1,64,2048]{2,1,0:T(8,128)(2,1)S(1)}, u32[]{:S(2)}, u32[]{:S(2)}) collective-permute-start(bf16[1,64,2048]{2,1,0:T(8,128)(2,1)S(1)} %get-tuple-element.50), channel_id=1, source_target_pairs={{0,1},{1,2},{2,3},{3,4},{4,5},{5,6},{6,7},{7,8},{8,9},{9,10},{10,1... | collective-permute-start | bytes 786440 | tf_op jit(solution)/shard_map/ppermute | solution.py:70
  263.9 104.3 %all-to-all-start.1 = ((bf16[16,64,2048]{2,1,0:T(8,128)(2,1)}), bf16[16,64,2048]{2,1,0:T(8,128)(2,1)}, u32[]{:S(2)}, u32[]{:S(2)}) async-start(bf16[16,64,2048]{2,1,0:T(8,128)(2,1)} %bitcast.216), calls=%async_computation.1 | async-start | bytes 8388608 | tf_op jit(solution)/shard_map/all_to_all | solution.py:57
  381.2 14.3 %collective-permute-start.16 = (bf16[1,64,2048]{2,1,0:T(8,128)(2,1)}, bf16[1,64,2048]{2,1,0:T(8,128)(2,1)}, u32[]{:S(2)}, u32[]{:S(2)}) collective-permute-start(bf16[1,64,2048]{2,1,0:T(8,128)(2,1)} %get-tuple-element.49), channel_id=1, source_target_pairs={{0,15},{1,0},{2,1},{3,2},{4,3},{5,4},{6,5},{7,6},{8,7},{9,8},{10,9... | collective-permute-start | bytes 786440 | tf_op jit(solution)/shard_map/ppermute | solution.py:70
  381.2 15.3 %collective-permute-start.17 = (bf16[1,64,2048]{2,1,0:T(8,128)(2,1)}, bf16[1,64,2048]{2,1,0:T(8,128)(2,1)}, u32[]{:S(2)}, u32[]{:S(2)}) collective-permute-start(bf16[1,64,2048]{2,1,0:T(8,128)(2,1)} %get-tuple-element.48), channel_id=1, source_target_pairs={{0,14},{1,15},{2,0},{3,1},{4,2},{5,3},{6,4},{7,5},{8,6},{9,7},{10,... | collective-permute-start | bytes 786440 | tf_op jit(solution)/shard_map/ppermute | solution.py:70
  382.0 18.3 %collective-permute-start.18 = (bf16[1,64,2048]{2,1,0:T(8,128)(2,1)}, bf16[1,64,2048]{2,1,0:T(8,128)(2,1)S(1)}, u32[]{:S(2)}, u32[]{:S(2)}) collective-permute-start(bf16[1,64,2048]{2,1,0:T(8,128)(2,1)} %get-tuple-element.47), channel_id=1, source_target_pairs={{0,13},{1,14},{2,15},{3,0},{4,1},{5,2},{6,3},{7,4},{8,5},{9,6},{10... | collective-permute-start | bytes 786440 | tf_op jit(solution)/shard_map/ppermute | solution.py:70
  382.0 20.6 %collective-permute-start.19 = (bf16[1,64,2048]{2,1,0:T(8,128)(2,1)}, bf16[1,64,2048]{2,1,0:T(8,128)(2,1)S(1)}, u32[]{:S(2)}, u32[]{:S(2)}) collective-permute-start(bf16[1,64,2048]{2,1,0:T(8,128)(2,1)} %get-tuple-element.46), channel_id=1, source_target_pairs={{0,12},{1,13},{2,14},{3,15},{4,0},{5,1},{6,2},{7,3},{8,4},{9,5},{1... | collective-permute-start | bytes 786440 | tf_op jit(solution)/shard_map/ppermute | solution.py:70
  386.3 25.6 %collective-permute-start.20 = (bf16[1,64,2048]{2,1,0:T(8,128)(2,1)}, bf16[1,64,2048]{2,1,0:T(8,128)(2,1)S(1)}, u32[]{:S(2)}, u32[]{:S(2)}) collective-permute-start(bf16[1,64,2048]{2,1,0:T(8,128)(2,1)} %get-tuple-element.45), channel_id=1, source_target_pairs={{0,11},{1,12},{2,13},{3,14},{4,15},{5,0},{6,1},{7,2},{8,3},{9,4},{... | collective-permute-start | bytes 786440 | tf_op jit(solution)/shard_map/ppermute | solution.py:70
  395.6 52.9 %collective-permute-start.21 = (bf16[1,64,2048]{2,1,0:T(8,128)(2,1)}, bf16[1,64,2048]{2,1,0:T(8,128)(2,1)S(1)}, u32[]{:S(2)}, u32[]{:S(2)}) collective-permute-start(bf16[1,64,2048]{2,1,0:T(8,128)(2,1)} %get-tuple-element.44), channel_id=1, source_target_pairs={{0,10},{1,11},{2,12},{3,13},{4,14},{5,15},{6,0},{7,1},{8,2},{9,3},... | collective-permute-start | bytes 786440 | tf_op jit(solution)/shard_map/ppermute | solution.py:70
  396.5 52.0 %collective-permute-start.22 = (bf16[1,64,2048]{2,1,0:T(8,128)(2,1)}, bf16[1,64,2048]{2,1,0:T(8,128)(2,1)S(1)}, u32[]{:S(2)}, u32[]{:S(2)}) collective-permute-start(bf16[1,64,2048]{2,1,0:T(8,128)(2,1)} %get-tuple-element.43), channel_id=1, source_target_pairs={{0,9},{1,10},{2,11},{3,12},{4,13},{5,14},{6,15},{7,0},{8,1},{9,2},... | collective-permute-start | bytes 786440 | tf_op jit(solution)/shard_map/ppermute | solution.py:70
  400.3 48.4 %collective-permute-start.23 = (bf16[1,64,2048]{2,1,0:T(8,128)(2,1)}, bf16[1,64,2048]{2,1,0:T(8,128)(2,1)S(1)}, u32[]{:S(2)}, u32[]{:S(2)}) collective-permute-start(bf16[1,64,2048]{2,1,0:T(8,128)(2,1)} %get-tuple-element.42), channel_id=1, source_target_pairs={{0,8},{1,9},{2,10},{3,11},{4,12},{5,13},{6,14},{7,15},{8,0},{9,1},... | collective-permute-start | bytes 786440 | tf_op jit(solution)/shard_map/ppermute | solution.py:70
  402.7 65.2 %collective-permute-start.24 = (bf16[1,64,2048]{2,1,0:T(8,128)(2,1)}, bf16[1,64,2048]{2,1,0:T(8,128)(2,1)S(1)}, u32[]{:S(2)}, u32[]{:S(2)}) collective-permute-start(bf16[1,64,2048]{2,1,0:T(8,128)(2,1)} %get-tuple-element.41), channel_id=1, source_target_pairs={{0,7},{1,8},{2,9},{3,10},{4,11},{5,12},{6,13},{7,14},{8,15},{9,0},... | collective-permute-start | bytes 786440 | tf_op jit(solution)/shard_map/ppermute | solution.py:70
  411.8 61.7 %collective-permute-start.25 = (bf16[1,64,2048]{2,1,0:T(8,128)(2,1)}, bf16[1,64,2048]{2,1,0:T(8,128)(2,1)S(1)}, u32[]{:S(2)}, u32[]{:S(2)}) collective-permute-start(bf16[1,64,2048]{2,1,0:T(8,128)(2,1)} %get-tuple-element.40), channel_id=1, source_target_pairs={{0,6},{1,7},{2,8},{3,9},{4,10},{5,11},{6,12},{7,13},{8,14},{9,15},... | collective-permute-start | bytes 786440 | tf_op jit(solution)/shard_map/ppermute | solution.py:70
  448.5 32.3 %collective-permute-start.26 = (bf16[1,64,2048]{2,1,0:T(8,128)(2,1)}, bf16[1,64,2048]{2,1,0:T(8,128)(2,1)S(1)}, u32[]{:S(2)}, u32[]{:S(2)}) collective-permute-start(bf16[1,64,2048]{2,1,0:T(8,128)(2,1)} %get-tuple-element.39), channel_id=1, source_target_pairs={{0,5},{1,6},{2,7},{3,8},{4,9},{5,10},{6,11},{7,12},{8,13},{9,14},{... | collective-permute-start | bytes 786440 | tf_op jit(solution)/shard_map/ppermute | solution.py:70
  448.6 33.5 %collective-permute-start.27 = (bf16[1,64,2048]{2,1,0:T(8,128)(2,1)}, bf16[1,64,2048]{2,1,0:T(8,128)(2,1)S(1)}, u32[]{:S(2)}, u32[]{:S(2)}) collective-permute-start(bf16[1,64,2048]{2,1,0:T(8,128)(2,1)} %get-tuple-element.38), channel_id=1, source_target_pairs={{0,4},{1,5},{2,6},{3,7},{4,8},{5,9},{6,10},{7,11},{8,12},{9,13},{1... | collective-permute-start | bytes 786440 | tf_op jit(solution)/shard_map/ppermute | solution.py:70
  448.7 33.4 %collective-permute-start.28 = (bf16[1,64,2048]{2,1,0:T(8,128)(2,1)}, bf16[1,64,2048]{2,1,0:T(8,128)(2,1)S(1)}, u32[]{:S(2)}, u32[]{:S(2)}) collective-permute-start(bf16[1,64,2048]{2,1,0:T(8,128)(2,1)} %get-tuple-element.37), channel_id=1, source_target_pairs={{0,3},{1,4},{2,5},{3,6},{4,7},{5,8},{6,9},{7,10},{8,11},{9,12},{10... | collective-permute-start | bytes 786440 | tf_op jit(solution)/shard_map/ppermute | solution.py:70
  467.9 18.7 %collective-permute-start.29 = (bf16[1,64,2048]{2,1,0:T(8,128)(2,1)S(1)}, bf16[1,64,2048]{2,1,0:T(8,128)(2,1)S(1)}, u32[]{:S(2)}, u32[]{:S(2)}) collective-permute-start(bf16[1,64,2048]{2,1,0:T(8,128)(2,1)S(1)} %copy-done.8), channel_id=1, source_target_pairs={{0,2},{1,3},{2,4},{3,5},{4,6},{5,7},{6,8},{7,9},{8,10},{9,11},{10,... | collective-permute-start | bytes 786440 | tf_op jit(solution)/shard_map/ppermute | solution.py:70
  473.5 17.4 %collective-permute-start.30 = (bf16[1,64,2048]{2,1,0:T(8,128)(2,1)S(1)}, bf16[1,64,2048]{2,1,0:T(8,128)(2,1)S(1)}, u32[]{:S(2)}, u32[]{:S(2)}) collective-permute-start(bf16[1,64,2048]{2,1,0:T(8,128)(2,1)S(1)} %get-tuple-element.35), channel_id=1, source_target_pairs={{0,1},{1,2},{2,3},{3,4},{4,5},{5,6},{6,7},{7,8},{8,9},{9,10},{10,1... | collective-permute-start | bytes 786440 | tf_op jit(solution)/shard_map/ppermute | solution.py:70
  518.4 106.9 %all-to-all-start.2 = ((bf16[16,64,2048]{2,1,0:T(8,128)(2,1)}), bf16[16,64,2048]{2,1,0:T(8,128)(2,1)}, u32[]{:S(2)}, u32[]{:S(2)}) async-start(bf16[16,64,2048]{2,1,0:T(8,128)(2,1)} %bitcast.215), calls=%async_computation.2 | async-start | bytes 8388608 | tf_op jit(solution)/shard_map/all_to_all | solution.py:57
  529.7 231.8 %collective-permute-start.31 = (bf16[64,2048]{1,0:T(8,128)(2,1)}, bf16[64,2048]{1,0:T(8,128)(2,1)}, u32[]{:S(2)}, u32[]{:S(2)}) collective-permute-start(bf16[64,2048]{1,0:T(8,128)(2,1)} %fusion.51), channel_id=1, source_target_pairs={{16,0},{17,1},{18,2},{19,3},{20,4},{21,5},{22,6},{23,7},{24,8},{25... | collective-permute-start | bytes 786440 | tf_op jit(solution)/shard_map/ppermute | solution.py:14
  638.5 14.4 %collective-permute-start.33 = (bf16[1,64,2048]{2,1,0:T(8,128)(2,1)}, bf16[1,64,2048]{2,1,0:T(8,128)(2,1)}, u32[]{:S(2)}, u32[]{:S(2)}) collective-permute-start(bf16[1,64,2048]{2,1,0:T(8,128)(2,1)} %get-tuple-element.34), channel_id=1, source_target_pairs={{0,15},{1,0},{2,1},{3,2},{4,3},{5,4},{6,5},{7,6},{8,7},{9,8},{10,9... | collective-permute-start | bytes 786440 | tf_op jit(solution)/shard_map/ppermute | solution.py:70
  638.5 15.4 %collective-permute-start.34 = (bf16[1,64,2048]{2,1,0:T(8,128)(2,1)}, bf16[1,64,2048]{2,1,0:T(8,128)(2,1)}, u32[]{:S(2)}, u32[]{:S(2)}) collective-permute-start(bf16[1,64,2048]{2,1,0:T(8,128)(2,1)} %get-tuple-element.33), channel_id=1, source_target_pairs={{0,14},{1,15},{2,0},{3,1},{4,2},{5,3},{6,4},{7,5},{8,6},{9,7},{10,... | collective-permute-start | bytes 786440 | tf_op jit(solution)/shard_map/ppermute | solution.py:70
  638.7 16.4 %collective-permute-start.35 = (bf16[1,64,2048]{2,1,0:T(8,128)(2,1)}, bf16[1,64,2048]{2,1,0:T(8,128)(2,1)S(1)}, u32[]{:S(2)}, u32[]{:S(2)}) collective-permute-start(bf16[1,64,2048]{2,1,0:T(8,128)(2,1)} %get-tuple-element.32), channel_id=1, source_target_pairs={{0,13},{1,14},{2,15},{3,0},{4,1},{5,2},{6,3},{7,4},{8,5},{9,6},{10... | collective-permute-start | bytes 786440 | tf_op jit(solution)/shard_map/ppermute | solution.py:70
  638.7 23.2 %collective-permute-start.36 = (bf16[1,64,2048]{2,1,0:T(8,128)(2,1)}, bf16[1,64,2048]{2,1,0:T(8,128)(2,1)S(1)}, u32[]{:S(2)}, u32[]{:S(2)}) collective-permute-start(bf16[1,64,2048]{2,1,0:T(8,128)(2,1)} %get-tuple-element.31), channel_id=1, source_target_pairs={{0,12},{1,13},{2,14},{3,15},{4,0},{5,1},{6,2},{7,3},{8,4},{9,5},{1... | collective-permute-start | bytes 786440 | tf_op jit(solution)/shard_map/ppermute | solution.py:70
  652.9 26.1 %collective-permute-start.37 = (bf16[1,64,2048]{2,1,0:T(8,128)(2,1)}, bf16[1,64,2048]{2,1,0:T(8,128)(2,1)S(1)}, u32[]{:S(2)}, u32[]{:S(2)}) collective-permute-start(bf16[1,64,2048]{2,1,0:T(8,128)(2,1)} %get-tuple-element.30), channel_id=1, source_target_pairs={{0,11},{1,12},{2,13},{3,14},{4,15},{5,0},{6,1},{7,2},{8,3},{9,4},{... | collective-permute-start | bytes 786440 | tf_op jit(solution)/shard_map/ppermute | solution.py:70
  653.9 25.2 %collective-permute-start.38 = (bf16[1,64,2048]{2,1,0:T(8,128)(2,1)}, bf16[1,64,2048]{2,1,0:T(8,128)(2,1)S(1)}, u32[]{:S(2)}, u32[]{:S(2)}) collective-permute-start(bf16[1,64,2048]{2,1,0:T(8,128)(2,1)} %get-tuple-element.29), channel_id=1, source_target_pairs={{0,10},{1,11},{2,12},{3,13},{4,14},{5,15},{6,0},{7,1},{8,2},{9,3},... | collective-permute-start | bytes 786440 | tf_op jit(solution)/shard_map/ppermute | solution.py:70
  655.1 42.2 %collective-permute-start.39 = (bf16[1,64,2048]{2,1,0:T(8,128)(2,1)}, bf16[1,64,2048]{2,1,0:T(8,128)(2,1)S(1)}, u32[]{:S(2)}, u32[]{:S(2)}) collective-permute-start(bf16[1,64,2048]{2,1,0:T(8,128)(2,1)} %get-tuple-element.28), channel_id=1, source_target_pairs={{0,9},{1,10},{2,11},{3,12},{4,13},{5,14},{6,15},{7,0},{8,1},{9,2},... | collective-permute-start | bytes 786440 | tf_op jit(solution)/shard_map/ppermute | solution.py:70
  661.9 55.1 %collective-permute-start.40 = (bf16[1,64,2048]{2,1,0:T(8,128)(2,1)}, bf16[1,64,2048]{2,1,0:T(8,128)(2,1)S(1)}, u32[]{:S(2)}, u32[]{:S(2)}) collective-permute-start(bf16[1,64,2048]{2,1,0:T(8,128)(2,1)} %get-tuple-element.27), channel_id=1, source_target_pairs={{0,8},{1,9},{2,10},{3,11},{4,12},{5,13},{6,14},{7,15},{8,0},{9,1},... | collective-permute-start | bytes 786440 | tf_op jit(solution)/shard_map/ppermute | solution.py:70
  679.0 38.1 %collective-permute-start.41 = (bf16[1,64,2048]{2,1,0:T(8,128)(2,1)}, bf16[1,64,2048]{2,1,0:T(8,128)(2,1)S(1)}, u32[]{:S(2)}, u32[]{:S(2)}) collective-permute-start(bf16[1,64,2048]{2,1,0:T(8,128)(2,1)} %get-tuple-element.26), channel_id=1, source_target_pairs={{0,7},{1,8},{2,9},{3,10},{4,11},{5,12},{6,13},{7,14},{8,15},{9,0},... | collective-permute-start | bytes 786440 | tf_op jit(solution)/shard_map/ppermute | solution.py:70
  679.1 38.1 %collective-permute-start.42 = (bf16[1,64,2048]{2,1,0:T(8,128)(2,1)}, bf16[1,64,2048]{2,1,0:T(8,128)(2,1)S(1)}, u32[]{:S(2)}, u32[]{:S(2)}) collective-permute-start(bf16[1,64,2048]{2,1,0:T(8,128)(2,1)} %get-tuple-element.25), channel_id=1, source_target_pairs={{0,6},{1,7},{2,8},{3,9},{4,10},{5,11},{6,12},{7,13},{8,14},{9,15},... | collective-permute-start | bytes 786440 | tf_op jit(solution)/shard_map/ppermute | solution.py:70
  697.3 37.4 %collective-permute-start.43 = (bf16[1,64,2048]{2,1,0:T(8,128)(2,1)}, bf16[1,64,2048]{2,1,0:T(8,128)(2,1)S(1)}, u32[]{:S(2)}, u32[]{:S(2)}) collective-permute-start(bf16[1,64,2048]{2,1,0:T(8,128)(2,1)} %get-tuple-element.24), channel_id=1, source_target_pairs={{0,5},{1,6},{2,7},{3,8},{4,9},{5,10},{6,11},{7,12},{8,13},{9,14},{... | collective-permute-start | bytes 786440 | tf_op jit(solution)/shard_map/ppermute | solution.py:70
  717.0 20.0 %collective-permute-start.44 = (bf16[1,64,2048]{2,1,0:T(8,128)(2,1)}, bf16[1,64,2048]{2,1,0:T(8,128)(2,1)S(1)}, u32[]{:S(2)}, u32[]{:S(2)}) collective-permute-start(bf16[1,64,2048]{2,1,0:T(8,128)(2,1)} %get-tuple-element.23), channel_id=1, source_target_pairs={{0,4},{1,5},{2,6},{3,7},{4,8},{5,9},{6,10},{7,11},{8,12},{9,13},{1... | collective-permute-start | bytes 786440 | tf_op jit(solution)/shard_map/ppermute | solution.py:70
  717.1 20.2 %collective-permute-start.45 = (bf16[1,64,2048]{2,1,0:T(8,128)(2,1)S(1)}, bf16[1,64,2048]{2,1,0:T(8,128)(2,1)S(1)}, u32[]{:S(2)}, u32[]{:S(2)}) collective-permute-start(bf16[1,64,2048]{2,1,0:T(8,128)(2,1)S(1)} %copy-done.10), channel_id=1, source_target_pairs={{0,3},{1,4},{2,5},{3,6},{4,7},{5,8},{6,9},{7,10},{8,11},{9,12},{10... | collective-permute-start | bytes 786440 | tf_op jit(solution)/shard_map/ppermute | solution.py:70
  717.2 25.7 %collective-permute-start.46 = (bf16[1,64,2048]{2,1,0:T(8,128)(2,1)S(1)}, bf16[1,64,2048]{2,1,0:T(8,128)(2,1)S(1)}, u32[]{:S(2)}, u32[]{:S(2)}) collective-permute-start(bf16[1,64,2048]{2,1,0:T(8,128)(2,1)S(1)} %copy-done.9), channel_id=1, source_target_pairs={{0,2},{1,3},{2,4},{3,5},{4,6},{5,7},{6,8},{7,9},{8,10},{9,11},{10,... | collective-permute-start | bytes 786440 | tf_op jit(solution)/shard_map/ppermute | solution.py:70
  (33 other events, 838.5 us)
